TPU v7x, 256 devices: a whole 4x4x8 slice. The times are simulated.
256 devices in a mesh: row: 8 (over y, core), leaf: 32 (over x, z).
Axes of the slice: x: 4, y: 4, z: 8, core: 2. Of those that a mesh axis runs over, the one named last changes fastest.
Arguments:
- diag_blocks: float32 [32, 24, 256, 256], P('leaf', 'row'), as said below
- panel: float32 [32, 24, 768, 256], P('leaf', None, 'row'), may hold values from -1.5 to 1.5
- parent: int32 [32, 24, 1], replicated, may hold values from 0 to 31; in each aligned block of 24 rows (0 to 23, 24 to 47, ..., all dimensions but the last counted through in order) at most 2 rows name the same one
- rel: int32 [32, 24, 6], replicated, may hold values from 0 to 7, as said below
- front: float32 [32, 1024, 1024], P('leaf', None, 'row'), may hold values from -6 to 6
Outputs:
- factor_diag: float32 [32, 24, 256, 256], P('leaf', 'row')
- factor_panel: bfloat16 [32, 24, 768, 256], P('leaf', None, 'row')
- new_front: float32 [32, 1024, 1024], P('leaf', None, 'row')
Inputs may be any that keep to these rules, and one draw needn't show every extreme that they name: Among the 24 supernodes of one leaf index at most 2 have the same parent owner, and some leaf index reaches 2. `rel`: the 6 entries of each supernode name different blocks of the parent's front, in rising order. `diag_blocks`: every block is symmetric positive definite.
All inputs are finite; a program needn't handle non-finite values.
Results may differ from a plain program's by a relative error of at most 0.0011.
Values may be sent and summed in bfloat16 or wider, within the bound.
No kernel may reach another device: no remote copies, remote signals or barrier semaphores. Data moves between devices by JAX's collectives and lax.ppermute only.
A program may use at most 128 MiB of HBM per device.

v0:
```python
import jax
import jax.numpy as jnp
from jax import lax
from jax.sharding import PartitionSpec as P

W = 256
BS = 128
FB = 8
P_SIZE = 6


def on_device(diag_blocks, panel, parent, rel, front):
    row_count = lax.axis_size("row")
    leaf_count = lax.axis_size("leaf")
    row_index = lax.axis_index("row")
    leaf_index = lax.axis_index("leaf")
    own_factor = jnp.linalg.cholesky(diag_blocks[0])
    factors_all = lax.all_gather(own_factor, "row", axis=0, tiled=True)
    solved = jax.scipy.linalg.solve_triangular(
        factors_all, jnp.swapaxes(panel[0], 1, 2), lower=True
    )
    panel_rows = jnp.swapaxes(solved, 1, 2).astype(jnp.bfloat16)
    owners = parent[:, :, 0]
    supernodes = owners.shape[1]
    most_slots = max(2, 3 * supernodes // (2 * leaf_count))
    node_ids = jnp.arange(supernodes, dtype=jnp.int32)
    before = node_ids[None, :] < node_ids[:, None]
    same_owner = owners[:, :, None] == owners[:, None, :]
    position = jnp.sum(jnp.logical_and(same_owner, before[None]), axis=2)
    slot_ids = jnp.arange(most_slots, dtype=jnp.int32)
    targets = jnp.arange(leaf_count, dtype=jnp.int32)
    my_owner = lax.dynamic_index_in_dim(owners, leaf_index, 0, keepdims=False)
    my_position = lax.dynamic_index_in_dim(position, leaf_index, 0, keepdims=False)
    send_match = jnp.logical_and(
        my_owner[None, None, :] == targets[:, None, None],
        my_position[None, None, :] == slot_ids[None, :, None],
    )
    send_child = jnp.sum(jnp.where(send_match, node_ids, 0), axis=2)
    send_valid = jnp.any(send_match, axis=2)
    recv_match = jnp.logical_and(
        owners[:, None, :] == leaf_index, position[:, None, :] == slot_ids[None, :, None]
    )
    recv_valid = jnp.any(recv_match, axis=2)
    recv_blocks = jnp.sum(jnp.where(recv_match[..., None], rel[:, None, :, :], 0), axis=2)
    blocks_per_row = FB // row_count
    owned_blocks = row_index * blocks_per_row + jnp.arange(blocks_per_row, dtype=jnp.int32)
    columns = blocks_per_row * BS
    full_panel = lax.all_gather(panel_rows, "row", axis=1, tiled=True)
    my_blocks = lax.dynamic_index_in_dim(rel, leaf_index, 0, keepdims=False)
    leading = full_panel.shape[:-2]
    selector = (my_blocks[..., None, :] == owned_blocks[:, None]).astype(jnp.bfloat16)
    parted = full_panel.reshape(leading + (P_SIZE, BS, W))
    picked = jnp.einsum(
        "...tp,...pbw->...tbw", selector, parted, preferred_element_type=jnp.float32
    ).astype(jnp.bfloat16)
    picked = picked.reshape(leading + (columns, W))
    child_updates = jnp.einsum(
        "...iw,...cw->...ic", full_panel, picked, preferred_element_type=jnp.float32
    ).astype(jnp.bfloat16)
    outgoing = jnp.where(
        send_valid[..., None, None],
        jnp.take(child_updates, send_child, axis=0),
        jnp.zeros((), jnp.bfloat16),
    )
    incoming = lax.all_to_all(outgoing, "leaf", split_axis=0, concat_axis=0, tiled=True)
    front_ids = jnp.arange(FB, dtype=jnp.int32)
    placing = jnp.logical_and(
        recv_blocks[..., None, :] == front_ids[:, None], recv_valid[..., None, None]
    ).astype(jnp.bfloat16)
    parted_updates = incoming.reshape(incoming.shape[0], incoming.shape[1], P_SIZE, BS, columns)
    assembled = jnp.einsum(
        "smfp,smpic->fic", placing, parted_updates, preferred_element_type=jnp.float32
    )
    new_front = front[0] - assembled.reshape(FB * BS, columns)
    return (own_factor[None], panel_rows[None], new_front[None])


def solution(mesh):
    in_specs = (
        P("leaf", "row", None, None),
        P("leaf", None, "row", None),
        P(),
        P(),
        P("leaf", None, "row"),
    )
    out_specs = (P("leaf", "row", None, None), P("leaf", None, "row", None), P("leaf", None, "row"))
    return jax.shard_map(
        on_device, mesh=mesh, in_specs=in_specs, out_specs=out_specs, check_vma=False
    )
```

profile of v0, /device:TPU:163, one launch (start us, length us, event | category | flops | bytes accessed | tf_op | source)
XLA Modules:
  0.0 1087.2 jit_solution(9359395064277232795)
XLA Ops:
  7.2 0.0 all-gather.3.cloned.1.call-start
  7.3 1.4 copy.66
  8.7 1.2 fusion.16
  10.0 35.2 %custom-call.17 = f32[3,128,128]{2,1,0:T(8,128)S(1)} custom-call(f32[3,128,128]{2,1,0:T(8,128)S(1)} %cholesky.122), custom_call_target="Cholesky" | custom-call | tf_op jit(solution)/shard_map/jit(cholesky)/cholesky | solution.py:17
  45.2 29.5 %custom-call.18 = f32[3,1,128,128]{2,3,1,0:T(8,128)S(1)} custom-call(f32[3,1,128,128]{3,2,1,0:T(8,128)S(1)} %select_bitcast_fusion), custom_call_target="InvertDiagBlocksLowerTriangular" | custom-call | tf_op jit(solution)/shard_map/jit(cholesky)/cholesky | solution.py:17
  74.7 0.1 cholesky.117
  74.7 0.3 constant_dynamic-update-slice_fusion.1
  75.1 0.5 convolution_subtract_fusion
  75.6 35.2 %custom-call.19 = f32[3,128,128]{2,1,0:T(8,128)S(1)} custom-call(f32[3,128,128]{2,1,0:T(8,128)S(1)} %convolution_subtract_fusion), custom_call_target="Cholesky" | custom-call | tf_op jit(solution)/shard_map/jit(cholesky)/cholesky | solution.py:17
  110.8 0.1 compare_reduce_fusion
  111.0 1.0 select_select_fusion.1
  112.1 0.0 all-gather.3.cloned.1.call-update
  112.1 0.0 all-gather.5.cloned.1.call-start
  112.1 45.1 %all-gather.3.cloned.1.call-done = f32[24,256,256]{2,1,0:T(8,128)} async-done(((f32[3,256,256]{2,1,0:T(8,128)}), f32[24,256,256]{2,1,0:T(8,128)}) %all-gather.3.cloned.1.call-update) | async-done | bytes 6291472 | tf_op jit(solution)/shard_map/all_gather | solution.py:18
  157.3 6.3 broadcast_select_fusion
  163.6 0.1 triangular_solve.48
  163.7 0.0 copy-start.2
  163.7 10.5 while.1
  163.7 0.6 fusion.41
  164.3 5.0 bitcast_dynamic-update-slice_fusion.2
  169.3 0.6 fusion.41
  169.8 4.4 bitcast_dynamic-update-slice_fusion.2
  174.2 473.0 %custom-call.20 = f32[24,2,128,128]{2,3,1,0:T(8,128)} custom-call(f32[24,2,128,128]{3,2,1,0:T(8,128)} %bitcast.90), custom_call_target="InvertDiagBlocksLowerTriangular" | custom-call | tf_op jit(solution)/shard_map/jit(_solve_triangular)/vmap()/triangular_solve | solution.py:19
  647.2 0.0 copy-done.2
  647.2 2.9 fusion.32
  650.1 0.0 copy-start.1
  650.1 4.9 fusion.8
  655.1 0.0 copy-done.1
  655.1 1.5 fusion.11
  656.6 0.0 copy-start.5
  656.7 0.0 copy-start.4
  656.7 1.7 fusion.18
  658.4 0.0 all-gather.5.cloned.1.call-update
  658.4 0.0 copy-done.5
  658.4 0.2 convert_reduce_fusion
  658.6 0.2 dynamic-slice_reduce_fusion
  658.8 0.6 dynamic-slice_reduce_fusion.1
  659.4 0.1 iota_compare_fusion.5
  659.5 0.1 fusion.25
  659.6 0.1 copy.74
  659.7 0.1 and_reduce_fusion
  659.8 0.1 copy.73
  659.9 0.1 copy.76
  660.0 0.1 reshape.180
  660.1 0.0 copy-done.4
  660.1 0.1 constant_dynamic-slice_fusion.1
  660.2 0.1 copy.90
  660.3 0.1 copy.82
  660.5 54.8 %all-gather.5.cloned.1.call-done = bf16[24,768,256]{2,1,0:T(8,128)(2,1)} async-done(((bf16[24,96,256]{2,1,0:T(8,128)(2,1)}), bf16[24,768,256]{2,1,0:T(8,128)(2,1)}) %all-gather.5.cloned.1.call-update) | async-done | bytes 9437200 | tf_op jit(solution)/shard_map/all_gather | solution.py:48
  715.3 0.0 copy-start
  715.3 11.9 %fusion = bf16[24,1,128,256]{3,1,2,0:T(2,128)(2,1)} fusion(pred[24,6,1,1]{1,2,3,0:T(4,128)(4,1)S(1)} %copy.82, bf16[24,6,128,256]{3,2,1,0:T(8,128)(2,1)} %bitcast.84), kind=kOutput, calls=%fused_computation.3 | convolution fusion | flops 9437184 | bytes 11010192 | tf_op jit(solution)/shard_map/...tp,...pbw->...tbw/dot_general | solution.py:53
  727.2 0.0 copy-done
  727.2 6.1 convolution_convert_fusion
  733.3 9.5 gather_fusion
  742.8 11.0 %select_select_fusion = bf16[32,2,768,128]{3,2,1,0:T(8,128)(2,1)} fusion(bf16[32,2,768,128]{3,2,1,0:T(8,128)(2,1)} %bitcast.83, pred[32,2]{1,0:T(8,128)(4,1)S(1)} %copy.74, pred[32,2]{1,0:T(8,128)(4,1)S(1)} %copy.73), kind=kLoop, calls=%fused_computation.7 | loop fusion | flops 12582912 | bytes 25165952 | tf_op jit(solution)/shard_map/jit(_where)/select_n | solution.py:60
  753.9 9.2 all-to-all-start
  763.1 1.0 fusion.39
  764.2 302.4 %all-to-all-done = bf16[32,2,768,128]{3,2,1,0:T(8,128)(2,1)} async-done(((bf16[32,2,768,128]{3,2,1,0:T(8,128)(2,1)}), bf16[32,2,768,128]{3,2,1,0:T(8,128)(2,1)}, u32[]{:S(2)}, u32[]{:S(2)}) %all-to-all-start) | async-done | bytes 12582944 | tf_op jit(solution)/shard_map/all_to_all | solution.py:65
  1066.6 0.0 copy-start.3
  1066.6 12.8 %fusion.12 = f32[8,128,128]{2,0,1:T(8,128)S(1)} fusion(bf16[32,2,6,128,128]{4,3,2,1,0:T(8,128)(2,1)} %bitcast.24, s32[32,2,6]{0,2,1:T(8,128)S(1)} %select_reduce_fusion.2, pred[32,2]{0,1:T(4,128)(4,1)S(1)} %get-tuple-element.21), kind=kOutput, calls=%fused_computation.19 | convolution fusion | flops 100669440 | bytes 13108800 | tf_op jit(solution)/shard_map/smfp,smpic->fic/dot_general | solution.py:71
  1079.4 0.1 copy.78
  1079.5 0.0 copy-done.3
  1079.5 0.9 bitcast_subtract_fusion
  (20 shorter events, 0.3 us)
Async XLA Ops:
  7.2 150.1 %all-gather.3.cloned.1.call-start = ((), (), s32[]{:S(2)}) async-start(), calls=%async_computation.1 | async-start | bytes 7077888 | tf_op jit(solution)/shard_map/all_gather | solution.py:18
  112.1 603.2 %all-gather.5.cloned.1.call-start = ((), (), s32[]{:S(2)}) async-start(), calls=%async_computation.2 | async-start | bytes 10616832 | tf_op jit(solution)/shard_map/all_gather | solution.py:48
  163.7 483.5 %copy-start.2 = (f32[1,24,96,256]{3,2,1,0:T(8,128)S(1)}, f32[1,24,96,256]{3,2,1,0:T(8,128)}, u32[]{:S(2)}) copy-start(f32[1,24,96,256]{3,2,1,0:T(8,128)} %param.6) | copy-start | bytes 7077892
  650.1 5.0 copy-start.1
  656.6 1.8 copy-start.5
  656.7 3.4 copy-start.4
  715.3 11.9 %copy-start = (bf16[24,768,256]{2,1,0:T(8,128)(2,1)S(1)}, bf16[24,768,256]{2,1,0:T(8,128)(2,1)}, u32[]{:S(2)}) copy-start(bf16[24,768,256]{2,1,0:T(8,128)(2,1)} %all-gather.5.cloned.1.call-done) | copy-start | bytes 28311556
  753.9 312.7 %all-to-all-start = ((bf16[32,2,768,128]{3,2,1,0:T(8,128)(2,1)}), bf16[32,2,768,128]{3,2,1,0:T(8,128)(2,1)}, u32[]{:S(2)}, u32[]{:S(2)}) async-start(bf16[32,2,768,128]{3,2,1,0:T(8,128)(2,1)} %select_select_fusion), calls=%async_computation | async-start | bytes 25165824 | tf_op jit(solution)/shard_map/all_to_all | solution.py:65
  1066.6 12.9 %copy-start.3 = (f32[1,1024,128]{2,1,0:T(8,128)S(1)}, f32[1,1024,128]{2,1,0:T(8,128)}, u32[]{:S(2)}) copy-start(f32[1,1024,128]{2,1,0:T(8,128)} %param.9) | copy-start | bytes 1572868
Sparse Core Ops, SparseCore 0:
  112.2 45.0 all-gather.2
  658.5 56.7 all-gather.4
where the time goes:
time: 1090 us
  other arithmetic  597 us (55%)
  waiting for transfers between devices  402 us (37%)
  matrix products  41.1 us (4%)
  local copies, waits for them, and re-layouts  23.2 us (2%)
  between operations  14.3 us (1%)
    another operation x3, other arithmetic, on_device(): jax.scipy.linalg.solve_triangular(factors_all, jnp.swapaxes(panel[0], 1,...  479 us
    all_to_all x1, waiting for transfers between devices, on_device(): lax.all_to_all(outgoing, 'leaf', split_axis=0, concat_axis=0, tiled=True)  302 us
    another operation x9, other arithmetic, on_device(): own_factor = jnp.linalg.cholesky(diag_blocks[0])  100 us
    all_gather x1, waiting for transfers between devices, on_device(): full_panel = lax.all_gather(panel_rows, 'row', axis=1, tiled=True)  54.8 us
    all_gather x1, waiting for transfers between devices, on_device(): factors_all = lax.all_gather(own_factor, 'row', axis=0, tiled=True)  45.1 us
  transfers between devices with their start and end apart: 3, of which 3 were waited for; matrix products, arithmetic and copies ran while one was open for 0% of the time, Pallas kernels for 0%

commit v1 on v0

--- a/solution.py
+++ b/solution.py
@@ -9,13 +9,31 @@
 P_SIZE = 6
 
 
+def in_order(blocks, dim):
+    blocks = jnp.moveaxis(blocks, 0, dim)
+    shape = blocks.shape
+    return blocks.reshape(*shape[:dim], shape[dim] * shape[dim + 1], *shape[dim + 2 :])
+
+
+def doubled(shard, axis):
+    size = lax.axis_size(axis)
+    tiles = shard[None]
+    for level in range(size.bit_length() - 1):
+        apart = 1 << level
+        other = lax.ppermute(tiles, axis, [(i, i ^ apart) for i in range(size)])
+        both = jnp.stack([tiles, other])
+        upper = lax.axis_index(axis) >> level & 1
+        tiles = jnp.where(upper == 0, both, both[::-1]).reshape(-1, *shard.shape)
+    return tiles
+
+
 def on_device(diag_blocks, panel, parent, rel, front):
     row_count = lax.axis_size("row")
     leaf_count = lax.axis_size("leaf")
     row_index = lax.axis_index("row")
     leaf_index = lax.axis_index("leaf")
     own_factor = jnp.linalg.cholesky(diag_blocks[0])
-    factors_all = lax.all_gather(own_factor, "row", axis=0, tiled=True)
+    factors_all = in_order(doubled(own_factor, "row"), 0)
     solved = jax.scipy.linalg.solve_triangular(
         factors_all, jnp.swapaxes(panel[0], 1, 2), lower=True
     )

time: 1090 us -> 1170 us (1.073)
  waiting for transfers between devices: 402 us -> 468 us
    ppermute x0 -> x3, waiting for transfers between devices: none -> 103 us  [doubled(): other = lax.ppermute(tiles, axis, [(i, i ^ apart) for i in range(size)])]
    all_gather x1 -> x0, waiting for transfers between devices: 45.1 us -> none  [on_device(): factors_all = lax.all_gather(own_factor, 'row', axis=0, tiled=True)]
  transfers between devices with their start and end apart: 3 -> 5, of which waited for: 3 -> 5; matrix products, arithmetic and copies ran while one was open for 0% -> 0% of each run, Pallas kernels for 0% -> 0%
where the time goes in v1:
time: 1170 us; the launch traced here: 1160 us
  other arithmetic  597 us (51%)
  waiting for transfers between devices  468 us (40%)
  matrix products  39 us (3%)
  local copies, waits for them, and re-layouts  23 us (2%)
  starting transfers between devices  15.2 us (1%)
  between operations  14.6 us (1%)
    another operation x3, other arithmetic, on_device(): jax.scipy.linalg.solve_triangular(factors_all, jnp.swapaxes(panel[0], 1,...  476 us
    all_to_all x1, waiting for transfers between devices, on_device(): lax.all_to_all(outgoing, 'leaf', split_axis=0, concat_axis=0, tiled=True)  307 us
    ppermute x3, waiting for transfers between devices, doubled(): other = lax.ppermute(tiles, axis, [(i, i ^ apart) for i in range(size)])  103 us
    another operation x9, other arithmetic, on_device(): own_factor = jnp.linalg.cholesky(diag_blocks[0])  100 us
    all_gather x1, waiting for transfers between devices, on_device(): full_panel = lax.all_gather(panel_rows, 'row', axis=1, tiled=True)  57.8 us
  transfers between devices with their start and end apart: 5, of which 5 were waited for; matrix products, arithmetic and copies ran while one was open for 0% of the time, Pallas kernels for 0%

profile of v1, /device:TPU:163, one launch (start us, length us, event | category | flops | bytes accessed | tf_op | source)
XLA Modules:
  0.0 1157.5 jit_solution(17776389618895019812)
XLA Ops:
  7.2 0.0 all-gather.2.cloned.1.call-start
  7.3 1.4 copy.50
  8.7 1.2 fusion.18
  10.0 35.2 %custom-call.17 = f32[3,128,128]{2,1,0:T(8,128)S(1)} custom-call(f32[3,128,128]{2,1,0:T(8,128)S(1)} %cholesky.122), custom_call_target="Cholesky" | custom-call | tf_op jit(solution)/shard_map/jit(cholesky)/cholesky | solution.py:35
  45.2 29.5 %custom-call.18 = f32[3,1,128,128]{2,3,1,0:T(8,128)S(1)} custom-call(f32[3,1,128,128]{3,2,1,0:T(8,128)S(1)} %select_bitcast_fusion), custom_call_target="InvertDiagBlocksLowerTriangular" | custom-call | tf_op jit(solution)/shard_map/jit(cholesky)/cholesky | solution.py:35
  74.7 0.1 cholesky.117
  74.7 0.4 constant_dynamic-update-slice_fusion.1
  75.1 0.5 convolution_subtract_fusion
  75.6 35.2 %custom-call.19 = f32[3,128,128]{2,1,0:T(8,128)S(1)} custom-call(f32[3,128,128]{2,1,0:T(8,128)S(1)} %convolution_subtract_fusion), custom_call_target="Cholesky" | custom-call | tf_op jit(solution)/shard_map/jit(cholesky)/cholesky | solution.py:35
  110.8 0.1 compare_reduce_fusion
  111.0 0.2 fusion.21
  111.2 0.0 copy-start.2
  111.2 1.2 collective-permute-start
  112.5 1.9 collective-permute-done
  114.4 0.1 pad_maximum_fusion.2
  114.5 0.3 fusion.12
  114.8 1.4 collective-permute-start.1
  116.2 34.4 %collective-permute-done.1 = f32[2,3,256,256]{3,2,1,0:T(8,128)} collective-permute-done((f32[2,3,256,256]{3,2,1,0:T(8,128)S(1)}, f32[2,3,256,256]{3,2,1,0:T(8,128)}, u32[]{:S(2)}, u32[]{:S(2)}) %collective-permute-start.1) | collective-permute-done | bytes 1572896 | tf_op jit(solution)/shard_map/ppermute | solution.py:23
  150.6 1.7 pad_maximum_fusion.1
  152.3 0.3 reverse_select_fusion.1
  152.6 3.0 collective-permute-start.2
  155.6 67.1 %collective-permute-done.2 = f32[4,3,256,256]{3,2,1,0:T(8,128)} collective-permute-done((f32[4,3,256,256]{3,2,1,0:T(8,128)S(1)}, f32[4,3,256,256]{3,2,1,0:T(8,128)}, u32[]{:S(2)}, u32[]{:S(2)}) %collective-permute-start.2) | collective-permute-done | bytes 3145760 | tf_op jit(solution)/shard_map/ppermute | solution.py:23
  222.7 2.5 pad_maximum_fusion
  225.2 0.6 reverse_select_fusion
  225.8 3.9 bitcast_select_fusion
  229.8 0.1 triangular_solve.48
  229.9 10.4 while.1
  229.9 0.6 fusion.44
  230.5 4.9 bitcast_dynamic-update-slice_fusion.2
  235.3 0.6 fusion.44
  235.9 4.4 bitcast_dynamic-update-slice_fusion.2
  240.3 472.3 %custom-call.20 = f32[24,2,128,128]{2,3,1,0:T(8,128)S(1)} custom-call(f32[24,2,128,128]{3,2,1,0:T(8,128)} %bitcast.106), custom_call_target="InvertDiagBlocksLowerTriangular" | custom-call | tf_op jit(solution)/shard_map/jit(_solve_triangular)/vmap()/triangular_solve | solution.py:37
  712.6 0.0 copy-start.1
  712.6 2.9 fusion.36
  715.5 4.8 fusion.8
  720.3 1.5 fusion.13
  721.9 0.0 copy-start.5
  721.9 0.0 copy-start.4
  721.9 1.7 fusion.20
  723.6 0.0 all-gather.2.cloned.1.call-update
  723.6 0.0 copy-done.5
  723.7 0.2 convert_reduce_fusion
  723.8 0.2 dynamic-slice_reduce_fusion
  724.0 0.6 dynamic-slice_reduce_fusion.1
  724.6 0.1 iota_compare_fusion.5
  724.7 0.1 fusion.29
  724.8 0.1 copy.58
  724.9 0.1 and_reduce_fusion
  725.0 0.1 copy.57
  725.1 0.1 copy.60
  725.2 0.1 reshape.188
  725.3 0.1 constant_dynamic-slice_fusion.1
  725.4 0.1 copy.74
  725.5 0.1 copy.66
  725.7 57.8 %all-gather.2.cloned.1.call-done = bf16[24,768,256]{2,1,0:T(8,128)(2,1)} async-done(((bf16[24,96,256]{2,1,0:T(8,128)(2,1)}), bf16[24,768,256]{2,1,0:T(8,128)(2,1)}) %all-gather.2.cloned.1.call-update) | async-done | bytes 9437200 | tf_op jit(solution)/shard_map/all_gather | solution.py:66
  783.4 11.8 %fusion = bf16[24,1,128,256]{3,1,2,0:T(2,128)(2,1)S(1)} fusion(pred[24,6,1,1]{1,2,3,0:T(4,128)(4,1)S(1)} %copy.66, bf16[24,6,128,256]{3,2,1,0:T(8,128)(2,1)} %bitcast.97), kind=kOutput, calls=%fused_computation.3 | convolution fusion | flops 9437184 | bytes 11010192 | tf_op jit(solution)/shard_map/...tp,...pbw->...tbw/dot_general | solution.py:71
  795.3 4.2 convolution_convert_fusion
  799.5 9.5 gather_fusion
  809.0 11.0 select_select_fusion
  820.0 9.6 all-to-all-start
  829.7 306.9 %all-to-all-done = bf16[32,2,768,128]{3,2,1,0:T(8,128)(2,1)} async-done(((bf16[32,2,768,128]{3,2,1,0:T(8,128)(2,1)}), bf16[32,2,768,128]{3,2,1,0:T(8,128)(2,1)}, u32[]{:S(2)}, u32[]{:S(2)}) %all-to-all-start) | async-done | bytes 12582944 | tf_op jit(solution)/shard_map/all_to_all | solution.py:83
  1136.6 12.8 %fusion.14 = f32[8,128,128]{2,0,1:T(8,128)S(1)} fusion(bf16[32,2,6,128,128]{4,3,2,1,0:T(8,128)(2,1)} %bitcast.33, s32[32,2,6]{0,2,1:T(8,128)S(1)} %select_reduce_fusion.2, pred[32,2]{0,1:T(4,128)(4,1)S(1)} %get-tuple-element.21), kind=kOutput, calls=%fused_computation.27 | convolution fusion | flops 100669440 | bytes 13108800 | tf_op jit(solution)/shard_map/smfp,smpic->fic/dot_general | solution.py:89
  1149.4 0.1 copy.62
  1149.5 0.9 bitcast_subtract_fusion
  (27 shorter events, 0.3 us)
Async XLA Ops:
  7.2 776.3 %all-gather.2.cloned.1.call-start = ((), (), s32[]{:S(2)}) async-start(), calls=%async_computation.1 | async-start | bytes 10616832 | tf_op jit(solution)/shard_map/all_gather | solution.py:66
  111.2 3.2 copy-start.2
  111.2 3.1 collective-permute-start
  114.8 35.8 %collective-permute-start.1 = (f32[2,3,256,256]{3,2,1,0:T(8,128)S(1)}, f32[2,3,256,256]{3,2,1,0:T(8,128)}, u32[]{:S(2)}, u32[]{:S(2)}) collective-permute-start(f32[2,3,256,256]{3,2,1,0:T(8,128)S(1)} %get-tuple-element.26), channel_id=1, source_target_pairs={{0,64},{32,96},{64,0},{96,32},{128,192},{160,224},{192,128},{224,1... | collective-permute-start | bytes 4718600 | tf_op jit(solution)/shard_map/ppermute | solution.py:23
  152.6 70.1 %collective-permute-start.2 = (f32[4,3,256,256]{3,2,1,0:T(8,128)S(1)}, f32[4,3,256,256]{3,2,1,0:T(8,128)}, u32[]{:S(2)}, u32[]{:S(2)}) collective-permute-start(f32[4,3,256,256]{3,2,1,0:T(8,128)S(1)} %bitcast.98), channel_id=1, source_target_pairs={{0,128},{32,160},{64,192},{96,224},{128,0},{160,32},{192,64},{224,... | collective-permute-start | bytes 9437192 | tf_op jit(solution)/shard_map/ppermute | solution.py:23
  712.6 3.0 copy-start.1
  721.9 1.8 copy-start.5
  721.9 3.4 copy-start.4
  783.4 11.8 %copy-start = (bf16[24,768,256]{2,1,0:T(8,128)(2,1)S(1)}, bf16[24,768,256]{2,1,0:T(8,128)(2,1)}, u32[]{:S(2)}) copy-start(bf16[24,768,256]{2,1,0:T(8,128)(2,1)} %all-gather.2.cloned.1.call-done) | copy-start | bytes 28311556
  820.0 316.6 %all-to-all-start = ((bf16[32,2,768,128]{3,2,1,0:T(8,128)(2,1)}), bf16[32,2,768,128]{3,2,1,0:T(8,128)(2,1)}, u32[]{:S(2)}, u32[]{:S(2)}) async-start(bf16[32,2,768,128]{3,2,1,0:T(8,128)(2,1)} %select_select_fusion), calls=%async_computation | async-start | bytes 25165824 | tf_op jit(solution)/shard_map/all_to_all | solution.py:83
  1136.6 12.9 %copy-start.3 = (f32[1,1024,128]{2,1,0:T(8,128)S(1)}, f32[1,1024,128]{2,1,0:T(8,128)}, u32[]{:S(2)}) copy-start(f32[1,1024,128]{2,1,0:T(8,128)} %param.9) | copy-start | bytes 1572868
Sparse Core Ops, SparseCore 0:
  723.7 59.6 all-gather.1
